TPU v7x, 256 devices: a whole 4x4x8 slice. The times are simulated.
256 devices in a mesh: row: 4 (over z_lo, core), col: 16 (over x, y), chan: 4 (over z_hi).
Axes of the slice: x: 4, y: 4, z: 8 (z_hi: 4, z_lo: 2; z = z_hi * 2 + z_lo), core: 2. Of those that a mesh axis runs over, the one named last changes fastest.
Arguments:
- pair: bfloat16 [1024, 1024, 128], P('row', 'col'), may hold values from -6 to 6
- pair_mask: int32 [1024, 1024], P('row', 'col'), may hold values 0 or 1
- ln_gain: float32 [128], replicated, may hold values from 0.1 to 1.9
- ln_bias: float32 [128], replicated, may hold values from -3 to 3
- left_value: bfloat16 [128, 128], P(None, 'chan'), may hold values from -0.5 to 0.5
- left_gate: bfloat16 [128, 128], P(None, 'chan'), may hold values from -0.5 to 0.5
- right_value: bfloat16 [128, 128], P(None, 'chan'), may hold values from -0.5 to 0.5
- right_gate: bfloat16 [128, 128], P(None, 'chan'), may hold values from -0.5 to 0.5
- hid_gain: float32 [128], replicated, may hold values from 0.1 to 1.9
- hid_bias: float32 [128], replicated, may hold values from -3 to 3
- out_weight: bfloat16 [128, 128], replicated, may hold values from -0.5 to 0.5
- out_gate: bfloat16 [128, 128], replicated, may hold values from -0.5 to 0.5
Outputs:
- update: bfloat16 [1024, 1024, 128], P('row', ('col', 'chan'))
All inputs are finite; a program needn't handle non-finite values. No bound on the sum of `pair_mask` on one device may be relied on, other than what follows from the above.
Results may differ from a plain program's by a relative error of at most 0.025.
Values may be sent and summed in bfloat16 or wider, within the bound.
No kernel may reach another device: no remote copies, remote signals or barrier semaphores. Data moves between devices by JAX's collectives and lax.ppermute only.
A program may use at most 128 MiB of HBM per device.

v0:
```python
import jax
import jax.numpy as jnp
from jax import lax
from jax.sharding import PartitionSpec as P


def on_device(
    pair,
    pair_mask,
    ln_gain,
    ln_bias,
    left_value,
    left_gate,
    right_value,
    right_gate,
    hid_gain,
    hid_bias,
    out_weight,
    out_gate,
):
    tile_cols = pair.shape[1]
    group_width = left_value.shape[1]
    out_cols = tile_cols // lax.axis_size("chan")
    group_index = lax.axis_index("chan")
    source = pair.astype(jnp.float32)
    centre = jnp.mean(source, axis=-1, keepdims=True)
    shifted = source - centre
    spread = jnp.mean(shifted * shifted, axis=-1, keepdims=True)
    normed = (shifted * lax.rsqrt(spread + 1e-05) * ln_gain + ln_bias).astype(jnp.bfloat16)
    weights = jnp.concatenate([left_value, left_gate, right_value, right_gate], axis=1)
    projected_all = jnp.einsum("ikc,cq->qik", normed, weights, preferred_element_type=jnp.float32)
    valid = pair_mask.astype(jnp.float32)[None, :, :]
    left = (
        jax.nn.sigmoid(projected_all[group_width : 2 * group_width])
        * projected_all[:group_width]
        * valid
    ).astype(jnp.bfloat16)
    right = (
        jax.nn.sigmoid(projected_all[3 * group_width :])
        * projected_all[2 * group_width : 3 * group_width]
        * valid
    ).astype(jnp.bfloat16)
    own_normed = lax.dynamic_slice_in_dim(normed, group_index * out_cols, out_cols, 1)
    gating = jax.nn.sigmoid(
        jnp.einsum("ijc,cd->ijd", own_normed, out_gate, preferred_element_type=jnp.float32)
    )
    right_all = lax.all_gather(right, "row", axis=1, tiled=True)
    product = lax.psum_scatter(
        jnp.einsum("hik,hjk->jhi", left, right_all, preferred_element_type=jnp.float32).astype(
            jnp.bfloat16
        ),
        "col",
        scatter_dimension=0,
        tiled=True,
    ).astype(jnp.float32)
    product = product.astype(jnp.bfloat16)
    widened = product.astype(jnp.float32)
    first_sums = jnp.sum(widened, axis=1)
    second_sums = jnp.sum(widened * widened, axis=1)
    first_sums, second_sums = (
        lax.psum(first_sums.astype(jnp.bfloat16), "chan").astype(jnp.float32),
        lax.psum(second_sums.astype(jnp.bfloat16), "chan").astype(jnp.float32),
    )
    total_width = group_width * lax.axis_size("chan")
    mean_hid = first_sums / total_width
    spread_hid = second_sums / total_width - mean_hid * mean_hid
    gain_part = lax.dynamic_slice_in_dim(hid_gain, group_index * group_width, group_width, 0)
    bias_part = lax.dynamic_slice_in_dim(hid_bias, group_index * group_width, group_width, 0)
    weight_rows = lax.dynamic_slice_in_dim(out_weight, group_index * group_width, group_width, 0)
    hidden = (
        (widened - mean_hid[:, None, :])
        * lax.rsqrt(spread_hid + 1e-05)[:, None, :]
        * gain_part[None, :, None]
        + bias_part[None, :, None]
    ).astype(jnp.bfloat16)
    mixed = lax.psum_scatter(
        jnp.einsum("jhi,hd->jid", hidden, weight_rows, preferred_element_type=jnp.float32).astype(
            jnp.bfloat16
        ),
        "chan",
        scatter_dimension=0,
        tiled=True,
    ).astype(jnp.float32)
    return (gating * jnp.transpose(mixed, (1, 0, 2))).astype(jnp.bfloat16)


def solution(mesh):
    return jax.shard_map(
        on_device,
        mesh=mesh,
        in_specs=(
            P("row", "col", None),
            P("row", "col"),
            P(),
            P(),
            P(None, "chan"),
            P(None, "chan"),
            P(None, "chan"),
            P(None, "chan"),
            P(),
            P(),
            P(),
            P(),
        ),
        out_specs=P("row", ("col", "chan"), None),
        check_vma=False,
    )
```

profile of v0, /device:TPU:1, one launch (start us, length us, event | category | flops | bytes accessed | tf_op | source)
XLA Modules:
  0.0 375.0 jit_solution(5184248092818221821)
XLA Ops:
  6.5 0.0 copy-start
  6.5 0.0 all-gather.2.cloned.1.call-start
  6.6 0.0 copy-start.1
  6.6 10.7 %convert_reduce_fusion = f32[256,64]{0,1:T(8,128)S(1)} fusion(bf16[256,64,128]{2,1,0:T(8,128)(2,1)} %param.12), kind=kLoop, calls=%fused_computation.2 | loop fusion | flops 4177920 | bytes 4259840 | tf_op jit(solution)/shard_map/reduce_sum | solution.py:26
  17.3 0.0 copy-done.1
  17.3 11.6 %fusion.2 = f32[256,64]{0,1:T(8,128)S(1)} fusion(f32[256,64]{0,1:T(8,128)S(1)} %broadcast_multiply_fusion, bf16[256,64,128]{2,1,0:T(8,128)(2,1)S(1)} %copy-done.1), kind=kLoop, calls=%fused_computation.5 | loop fusion | flops 8372224 | bytes 4325376 | tf_op jit(solution)/shard_map/reduce_sum | solution.py:28
  29.0 0.0 copy-done.3
  29.0 0.0 copy-done.9
  29.0 0.0 copy-done.8
  29.0 0.0 copy-start.4
  29.0 0.0 copy-start.5
  29.0 0.0 copy-start.6
  29.1 0.0 copy-start.7
  29.1 9.3 %fusion.5 = bf16[256,64,128]{2,0,1:T(8,128)(2,1)S(1)} fusion(f32[128]{0:T(128)S(1)} %copy-done.8, f32[128]{0:T(128)S(1)} %copy-done.9, f32[256,64]{0,1:T(8,128)S(1)} %add_rsqrt_fusion.1, f32[256,64]{0,1:T(8,128)S(1)} %broadcast_multiply_fusion, bf16[256,64,128]{2,1,0:T(8,128)(2,1)S(1)} %copy-done.1), kind=kLoop, calls=%fused_computation.8 | loop fusion | flops 12582912 | bytes 8520704 | tf_op jit(solution)/shard_map/convert_element_type | solution.py:29
  38.4 0.0 copy-done.4
  38.4 0.0 copy-done.5
  38.4 0.0 copy-done.6
  38.4 0.0 copy-done.7
  38.4 0.0 copy-start.2
  38.4 1.3 fusion.26
  39.7 0.7 copy-done.2
  40.3 2.4 fusion.13
  42.7 0.0 all-gather.2.cloned.1.call-update
  42.8 0.0 reduce-scatter.3.cloned.1.call-start
  42.8 53.4 %all-gather.2.cloned.1.call-done = bf16[32,1024,64]{1,0,2:T(8,128)(2,1)} async-done(((bf16[32,256,64]{1,0,2:T(8,128)(2,1)}), bf16[32,1024,64]{1,0,2:T(8,128)(2,1)}) %all-gather.2.cloned.1.call-update) | async-done | bytes 4194320 | tf_op jit(solution)/shard_map/all_gather | solution.py:47
  96.2 10.3 %convert_bitcast_fusion = bf16[1024,32,256]{2,0,1:T(8,128)(2,1)} fusion(bf16[32,1024,64]{1,0,2:T(8,128)(2,1)} %all-gather.2.cloned.1.call-done, bf16[32,256,64]{1,0,2:T(8,128)(2,1)S(1)} %get-tuple-element.7), kind=kOutput, calls=%fused_computation | convolution fusion | flops 1082130432 | bytes 22020096 | tf_op jit(solution)/shard_map/hik,hjk->jhi/dot_general | solution.py:49
  106.5 0.0 reduce-scatter.3.cloned.1.call-update
  106.5 0.0 all-reduce.3.cloned.1.call-start
  106.6 115.2 %reduce-scatter.3.cloned.1.call-done = bf16[64,32,256]{2,0,1:T(8,128)(2,1)} async-done(((bf16[1024,32,256]{2,0,1:T(8,128)(2,1)}), bf16[64,32,256]{2,0,1:T(8,128)(2,1)}) %reduce-scatter.3.cloned.1.call-update) | async-done | bytes 1048592 | tf_op jit(solution)/shard_map/reduce_scatter | solution.py:48
  221.8 2.1 fusion.11
  223.8 2.0 reduce_sum.41
  225.8 0.0 all-reduce.3.cloned.1.call-update
  225.8 0.3 reduce-scatter.5.cloned.1.call-start
  226.1 0.0 copy-done.11
  226.1 0.1 dynamic_slice.13
  226.2 0.0 copy-done.12
  226.2 0.1 dynamic_slice.14
  226.3 47.2 %all-reduce.3.cloned.1.call-done = (bf16[64,256]{1,0:T(8,128)(2,1)}, bf16[64,256]{1,0:T(8,128)(2,1)}) async-done(((bf16[64,256]{1,0:T(8,128)(2,1)}, bf16[64,256]{1,0:T(8,128)(2,1)}), (bf16[64,256]{1,0:T(8,128)(2,1)}, bf16[64,256]{1,0:T(8,128)(2,1)})) %all-reduce.3.cloned.1.call-update) | async-done | bytes 65552 | tf_op jit(solution)/shard_map/psum | solution.py:62
  273.5 0.8 convert_multiply_fusion.1
  274.3 1.6 fusion.10
  275.9 0.0 copy-done
  275.9 0.0 copy-start.10
  275.9 3.3 convolution_convert_fusion
  279.2 0.0 reduce-scatter.5.cloned.1.call-update
  279.2 85.3 %reduce-scatter.5.cloned.1.call-done = bf16[16,256,128]{2,1,0:T(8,128)(2,1)} async-done(((bf16[64,256,128]{2,1,0:T(8,128)(2,1)}), bf16[16,256,128]{2,1,0:T(8,128)(2,1)}) %reduce-scatter.5.cloned.1.call-update) | async-done | bytes 1048592 | tf_op jit(solution)/shard_map/reduce_scatter | solution.py:76
  364.5 0.0 copy-done.10
  364.5 2.2 fusion.22
  366.8 1.6 copy.17
  (8 shorter events, 0.0 us)
Async XLA Ops:
  6.5 269.4 %copy-start = (bf16[128,128]{1,0:T(8,128)(2,1)S(1)}, bf16[128,128]{1,0:T(8,128)(2,1)}, u32[]{:S(2)}) copy-start(bf16[128,128]{1,0:T(8,128)(2,1)} %param.22) | copy-start | bytes 98308
  6.5 22.4 %copy-start.3 = (s32[256,64]{0,1:T(8,128)S(1)}, s32[256,64]{0,1:T(8,128)}, u32[]{:S(2)}) copy-start(s32[256,64]{0,1:T(8,128)} %param.13) | copy-start | bytes 196612
  6.5 22.5 %copy-start.9 = (f32[128]{0:T(128)S(1)}, f32[128]{0:T(128)}, u32[]{:S(2)}) copy-start(f32[128]{0:T(128)} %param.14) | copy-start | bytes 1540
  6.5 22.5 %copy-start.8 = (f32[128]{0:T(128)S(1)}, f32[128]{0:T(128)}, u32[]{:S(2)}) copy-start(f32[128]{0:T(128)} %param.15) | copy-start | bytes 1540
  6.5 89.7 %all-gather.2.cloned.1.call-start = ((), (), s32[]{:S(2)}) async-start(), calls=%async_computation.2 | async-start | bytes 5242880 | tf_op jit(solution)/shard_map/all_gather | solution.py:47
  6.6 10.7 %copy-start.1 = (bf16[256,64,128]{2,1,0:T(8,128)(2,1)S(1)}, bf16[256,64,128]{2,1,0:T(8,128)(2,1)}, u32[]{:S(2)}) copy-start(bf16[256,64,128]{2,1,0:T(8,128)(2,1)} %param.12) | copy-start | bytes 12582916
  29.0 9.3 %copy-start.4 = (bf16[128,32]{0,1:T(8,128)(2,1)S(1)}, bf16[128,32]{0,1:T(8,128)(2,1)}, u32[]{:S(2)}) copy-start(bf16[128,32]{0,1:T(8,128)(2,1)} %param.19) | copy-start | bytes 24580
  29.0 9.3 %copy-start.5 = (bf16[128,32]{0,1:T(8,128)(2,1)S(1)}, bf16[128,32]{0,1:T(8,128)(2,1)}, u32[]{:S(2)}) copy-start(bf16[128,32]{0,1:T(8,128)(2,1)} %param.18) | copy-start | bytes 24580
  29.0 9.3 %copy-start.6 = (bf16[128,32]{0,1:T(8,128)(2,1)S(1)}, bf16[128,32]{0,1:T(8,128)(2,1)}, u32[]{:S(2)}) copy-start(bf16[128,32]{0,1:T(8,128)(2,1)} %param.17) | copy-start | bytes 24580
  29.1 9.3 %copy-start.7 = (bf16[128,32]{0,1:T(8,128)(2,1)S(1)}, bf16[128,32]{0,1:T(8,128)(2,1)}, u32[]{:S(2)}) copy-start(bf16[128,32]{0,1:T(8,128)(2,1)} %param.16) | copy-start | bytes 24580
  38.4 1.9 copy-start.2
  42.8 179.0 %reduce-scatter.3.cloned.1.call-start = ((), (), s32[]{:S(2)}) async-start(), calls=%async_computation.3 | async-start | bytes 17825792 | tf_op jit(solution)/shard_map/reduce_scatter | solution.py:48
  106.5 119.6 %copy-start.11 = (f32[128]{0:T(128)S(1)}, f32[128]{0:T(128)}, u32[]{:S(2)}) copy-start(f32[128]{0:T(128)} %param.20) | copy-start | bytes 1540
  106.5 119.7 %copy-start.12 = (f32[128]{0:T(128)S(1)}, f32[128]{0:T(128)}, u32[]{:S(2)}) copy-start(f32[128]{0:T(128)} %param.21) | copy-start | bytes 1540
  106.5 167.0 %all-reduce.3.cloned.1.call-start = ((), (), s32[]{:S(2)}) async-start(), calls=%async_computation.5 | async-start | bytes 131072 | tf_op jit(solution)/shard_map/psum | solution.py:62
  225.8 138.7 %reduce-scatter.5.cloned.1.call-start = ((), (), s32[]{:S(2)}) async-start(), calls=%async_computation.4 | async-start | bytes 5242880 | tf_op jit(solution)/shard_map/reduce_scatter | solution.py:76
  275.9 88.6 %copy-start.10 = (bf16[128,128]{1,0:T(8,128)(2,1)S(1)}, bf16[128,128]{1,0:T(8,128)(2,1)}, u32[]{:S(2)}) copy-start(bf16[128,128]{1,0:T(8,128)(2,1)} %param.23) | copy-start | bytes 98308
Sparse Core Ops, SparseCore 0:
  42.9 53.2 all-gather.1
  106.6 115.0 reduce-scatter.2
  226.0 47.4 all-reduce.2
  279.4 85.1 reduce-scatter.4
where the time goes:
time: 375 us
  waiting for transfers between devices  301 us (80%)
  other arithmetic  40.5 us (11%)
  matrix products  17 us (5%)
  between operations  13.3 us (4%)
    reduce_scatter x1, waiting for transfers between devices, on_device(): lax.psum_scatter(jnp.einsum('hik,hjk->jhi', left, right_all, preferred_el...  115 us
    reduce_scatter x1, waiting for transfers between devices, on_device(): lax.psum_scatter(jnp.einsum('jhi,hd->jid', hidden, weight_rows, preferred...  85.3 us
    all_gather x1, waiting for transfers between devices, on_device(): right_all = lax.all_gather(right, 'row', axis=1, tiled=True)  53.4 us
    psum x1, waiting for transfers between devices, on_device(): lax.psum(second_sums.astype(jnp.bfloat16), 'chan').astype(jnp.float32)  47.2 us
    reduce_sum x1, other arithmetic, on_device(): spread = jnp.mean(shifted * shifted, axis=-1, keepdims=True)  11.6 us
    reduce_sum x1, other arithmetic, on_device(): centre = jnp.mean(source, axis=-1, keepdims=True)  10.7 us
    dot_general x1, matrix products, on_device(): jnp.einsum('hik,hjk->jhi', left, right_all, preferred_element_type=jnp.fl...  10.3 us
    convert_element_type x1, other arithmetic, on_device(): (shifted * lax.rsqrt(spread + 1e-05) * ln_gain + ln_bias).astype(jnp.bflo...  9.28 us
  transfers between devices with their start and end apart: 4, of which 4 were waited for; matrix products, arithmetic and copies ran while one was open for 0% of the time, Pallas kernels for 0%

commit v1 on v0

--- a/solution.py
+++ b/solution.py
@@ -2,6 +2,7 @@
 import jax.numpy as jnp
 from jax import lax
 from jax.sharding import PartitionSpec as P
+from jax.lax import all_gather
 
 
 def on_device(
@@ -57,9 +58,10 @@
     widened = product.astype(jnp.float32)
     first_sums = jnp.sum(widened, axis=1)
     second_sums = jnp.sum(widened * widened, axis=1)
+    sources_all_balance = lambda z_in: jnp.sum(all_gather(z_in, "chan"), axis=0)
     first_sums, second_sums = (
         lax.psum(first_sums.astype(jnp.bfloat16), "chan").astype(jnp.float32),
-        lax.psum(second_sums.astype(jnp.bfloat16), "chan").astype(jnp.float32),
+        sources_all_balance(second_sums.astype(jnp.bfloat16)).astype(jnp.float32),
     )
     total_width = group_width * lax.axis_size("chan")
     mean_hid = first_sums / total_width

time: 375 us -> 356 us (0.949)
  waiting for transfers between devices: 301 us -> 256 us
  blocking collectives: 0 us -> 28 us
    psum x1 -> x0, waiting for transfers between devices: 47.2 us -> none  [on_device(): lax.psum(second_sums.astype(jnp.bfloat16), 'chan').astype(jnp.float32)]
    psum x0 -> x1, blocking collectives: none -> 14.7 us  [on_device(): lax.psum(first_sums.astype(jnp.bfloat16), 'chan').astype(jnp.float32)]
    all_gather x0 -> x1, blocking collectives: none -> 13.3 us  [on_device(): sources_all_balance = lambda z_in: jnp.sum(all_gather(z_in, 'chan'), axis=0)]
  transfers between devices with their start and end apart: 4 -> 3, of which waited for: 4 -> 3; matrix products, arithmetic and copies ran while one was open for 0% -> 0% of each run, Pallas kernels for 0% -> 0%
where the time goes in v1:
time: 356 us
  waiting for transfers between devices  256 us (72%)
  other arithmetic  38.5 us (11%)
  blocking collectives  28 us (8%)
  matrix products  17 us (5%)
  between operations  13.3 us (4%)
    reduce_scatter x1, waiting for transfers between devices, on_device(): lax.psum_scatter(jnp.einsum('hik,hjk->jhi', left, right_all, preferred_el...  114 us
    reduce_scatter x1, waiting for transfers between devices, on_device(): lax.psum_scatter(jnp.einsum('jhi,hd->jid', hidden, weight_rows, preferred...  87.8 us
    all_gather x1, waiting for transfers between devices, on_device(): right_all = lax.all_gather(right, 'row', axis=1, tiled=True)  53.4 us
    psum x1, blocking collectives, on_device(): lax.psum(first_sums.astype(jnp.bfloat16), 'chan').astype(jnp.float32)  14.7 us
    all_gather x1, blocking collectives, on_device(): sources_all_balance = lambda z_in: jnp.sum(all_gather(z_in, 'chan'), axis=0)  13.3 us
    reduce_sum x1, other arithmetic, on_device(): spread = jnp.mean(shifted * shifted, axis=-1, keepdims=True)  11.6 us
    reduce_sum x1, other arithmetic, on_device(): centre = jnp.mean(source, axis=-1, keepdims=True)  10.7 us
    dot_general x1, matrix products, on_device(): jnp.einsum('hik,hjk->jhi', left, right_all, preferred_element_type=jnp.fl...  10.3 us
  transfers between devices with their start and end apart: 3, of which 3 were waited for; matrix products, arithmetic and copies ran while one was open for 0% of the time, Pallas kernels for 0%

profile of v1, /device:TPU:1, one launch (start us, length us, event | category | flops | bytes accessed | tf_op | source)
XLA Modules:
  0.0 355.8 jit_solution(4830547148209230650)
XLA Ops:
  6.5 0.0 copy-start
  6.5 0.0 copy-start.3
  6.5 0.0 copy-start.9
  6.5 0.0 all-gather.3.cloned.1.call-start
  6.6 0.0 copy-start.1
  6.6 10.7 %convert_reduce_fusion = f32[256,64]{0,1:T(8,128)S(1)} fusion(bf16[256,64,128]{2,1,0:T(8,128)(2,1)} %param.12), kind=kLoop, calls=%fused_computation.2 | loop fusion | flops 4177920 | bytes 4259840 | tf_op jit(solution)/shard_map/reduce_sum | solution.py:27
  17.3 0.0 copy-done.1
  17.3 11.6 %fusion.2 = f32[256,64]{0,1:T(8,128)S(1)} fusion(f32[256,64]{0,1:T(8,128)S(1)} %broadcast_multiply_fusion, bf16[256,64,128]{2,1,0:T(8,128)(2,1)S(1)} %copy-done.1), kind=kLoop, calls=%fused_computation.5 | loop fusion | flops 8372224 | bytes 4325376 | tf_op jit(solution)/shard_map/reduce_sum | solution.py:29
  29.0 0.0 copy-done.3
  29.0 0.0 copy-done.9
  29.0 0.0 copy-done.8
  29.0 0.0 copy-start.4
  29.0 0.0 copy-start.5
  29.0 0.0 copy-start.6
  29.1 0.0 copy-start.7
  29.1 9.3 %fusion.5 = bf16[256,64,128]{2,0,1:T(8,128)(2,1)S(1)} fusion(f32[128]{0:T(128)S(1)} %copy-done.8, f32[128]{0:T(128)S(1)} %copy-done.9, f32[256,64]{0,1:T(8,128)S(1)} %add_rsqrt_fusion.1, f32[256,64]{0,1:T(8,128)S(1)} %broadcast_multiply_fusion, bf16[256,64,128]{2,1,0:T(8,128)(2,1)S(1)} %copy-done.1), kind=kLoop, calls=%fused_computation.8 | loop fusion | flops 12582912 | bytes 8520704 | tf_op jit(solution)/shard_map/convert_element_type | solution.py:30
  38.4 0.0 copy-done.4
  38.4 0.0 copy-done.5
  38.4 0.0 copy-done.6
  38.4 0.0 copy-done.7
  38.4 0.0 copy-start.2
  38.4 1.3 fusion.26
  39.7 0.7 copy-done.2
  40.3 2.4 fusion.13
  42.7 0.0 all-gather.3.cloned.1.call-update
  42.8 0.0 reduce-scatter.3.cloned.1.call-start
  42.8 53.4 %all-gather.3.cloned.1.call-done = bf16[32,1024,64]{1,0,2:T(8,128)(2,1)} async-done(((bf16[32,256,64]{1,0,2:T(8,128)(2,1)}), bf16[32,1024,64]{1,0,2:T(8,128)(2,1)}) %all-gather.3.cloned.1.call-update) | async-done | bytes 4194320 | tf_op jit(solution)/shard_map/all_gather | solution.py:48
  96.2 10.3 %convert_bitcast_fusion = bf16[1024,32,256]{2,0,1:T(8,128)(2,1)} fusion(bf16[32,1024,64]{1,0,2:T(8,128)(2,1)} %all-gather.3.cloned.1.call-done, bf16[32,256,64]{1,0,2:T(8,128)(2,1)S(1)} %get-tuple-element.5), kind=kOutput, calls=%fused_computation | convolution fusion | flops 1082130432 | bytes 22020096 | tf_op jit(solution)/shard_map/hik,hjk->jhi/dot_general | solution.py:50
  106.5 0.0 reduce-scatter.3.cloned.1.call-update
  106.5 0.0 reduce-scatter.5.cloned.1.call-start
  106.5 0.6 copy-done.11
  107.1 0.1 dynamic_slice.13
  107.2 0.0 copy-done.12
  107.2 0.1 dynamic_slice.14
  107.3 114.5 %reduce-scatter.3.cloned.1.call-done = bf16[64,32,256]{2,0,1:T(8,128)(2,1)} async-done(((bf16[1024,32,256]{2,0,1:T(8,128)(2,1)}), bf16[64,32,256]{2,0,1:T(8,128)(2,1)}) %reduce-scatter.3.cloned.1.call-update) | async-done | bytes 1048592 | tf_op jit(solution)/shard_map/reduce_scatter | solution.py:49
  221.7 1.4 fusion.11
  223.2 13.3 %all-gather = bf16[256,256]{1,0:T(8,128)(2,1)S(1)} all-gather(bf16[64,256]{1,0:T(8,128)(2,1)S(1)} %fusion.11), channel_id=2, replica_groups=mesh['row'=4,'col'=16,'chan'=4] {'chan'}, dimensions={0}, use_global_device_ids=true | all-gather | bytes 163840 | tf_op jit(solution)/shard_map/all_gather | solution.py:61
  236.5 1.4 reduce_sum.53
  237.8 14.7 %psum.7 = bf16[64,256]{1,0:T(8,128)(2,1)S(1)} all-reduce(bf16[64,256]{1,0:T(8,128)(2,1)S(1)} %reduce_sum.53), channel_id=1, replica_groups=mesh['row'=4,'col'=16,'chan'=4] {'chan'}, use_global_device_ids=true, to_apply=%region_4.0 | all-reduce | flops 16384 | bytes 65536 | tf_op jit(solution)/shard_map/psum | solution.py:63
  252.6 1.6 fusion.10
  254.2 0.0 copy-done
  254.3 0.0 copy-start.10
  254.3 3.3 convolution_convert_fusion
  257.5 0.0 reduce-scatter.5.cloned.1.call-update
  257.6 87.8 %reduce-scatter.5.cloned.1.call-done = bf16[16,256,128]{2,1,0:T(8,128)(2,1)} async-done(((bf16[64,256,128]{2,1,0:T(8,128)(2,1)}), bf16[16,256,128]{2,1,0:T(8,128)(2,1)}) %reduce-scatter.5.cloned.1.call-update) | async-done | bytes 1048592 | tf_op jit(solution)/shard_map/reduce_scatter | solution.py:78
  345.3 0.0 copy-done.10
  345.3 2.2 fusion.22
  347.6 1.6 copy.22
  (8 shorter events, 0.1 us)
Async XLA Ops:
  6.5 247.7 %copy-start = (bf16[128,128]{1,0:T(8,128)(2,1)S(1)}, bf16[128,128]{1,0:T(8,128)(2,1)}, u32[]{:S(2)}) copy-start(bf16[128,128]{1,0:T(8,128)(2,1)} %param.22) | copy-start | bytes 98308
  6.5 22.4 %copy-start.3 = (s32[256,64]{0,1:T(8,128)S(1)}, s32[256,64]{0,1:T(8,128)}, u32[]{:S(2)}) copy-start(s32[256,64]{0,1:T(8,128)} %param.13) | copy-start | bytes 196612
  6.5 22.5 %copy-start.9 = (f32[128]{0:T(128)S(1)}, f32[128]{0:T(128)}, u32[]{:S(2)}) copy-start(f32[128]{0:T(128)} %param.14) | copy-start | bytes 1540
  6.5 22.5 %copy-start.8 = (f32[128]{0:T(128)S(1)}, f32[128]{0:T(128)}, u32[]{:S(2)}) copy-start(f32[128]{0:T(128)} %param.15) | copy-start | bytes 1540
  6.5 89.7 %all-gather.3.cloned.1.call-start = ((), (), s32[]{:S(2)}) async-start(), calls=%async_computation.2 | async-start | bytes 5242880 | tf_op jit(solution)/shard_map/all_gather | solution.py:48
  6.6 10.7 %copy-start.1 = (bf16[256,64,128]{2,1,0:T(8,128)(2,1)S(1)}, bf16[256,64,128]{2,1,0:T(8,128)(2,1)}, u32[]{:S(2)}) copy-start(bf16[256,64,128]{2,1,0:T(8,128)(2,1)} %param.12) | copy-start | bytes 12582916
  29.0 9.3 %copy-start.4 = (bf16[128,32]{0,1:T(8,128)(2,1)S(1)}, bf16[128,32]{0,1:T(8,128)(2,1)}, u32[]{:S(2)}) copy-start(bf16[128,32]{0,1:T(8,128)(2,1)} %param.19) | copy-start | bytes 24580
  29.0 9.3 %copy-start.5 = (bf16[128,32]{0,1:T(8,128)(2,1)S(1)}, bf16[128,32]{0,1:T(8,128)(2,1)}, u32[]{:S(2)}) copy-start(bf16[128,32]{0,1:T(8,128)(2,1)} %param.18) | copy-start | bytes 24580
  29.0 9.3 %copy-start.6 = (bf16[128,32]{0,1:T(8,128)(2,1)S(1)}, bf16[128,32]{0,1:T(8,128)(2,1)}, u32[]{:S(2)}) copy-start(bf16[128,32]{0,1:T(8,128)(2,1)} %param.17) | copy-start | bytes 24580
  29.1 9.3 %copy-start.7 = (bf16[128,32]{0,1:T(8,128)(2,1)S(1)}, bf16[128,32]{0,1:T(8,128)(2,1)}, u32[]{:S(2)}) copy-start(bf16[128,32]{0,1:T(8,128)(2,1)} %param.16) | copy-start | bytes 24580
  38.4 1.9 copy-start.2
  42.8 179.0 %reduce-scatter.3.cloned.1.call-start = ((), (), s32[]{:S(2)}) async-start(), calls=%async_computation.3 | async-start | bytes 17825792 | tf_op jit(solution)/shard_map/reduce_scatter | solution.py:49
  106.5 0.7 copy-start.11
  106.5 0.7 copy-start.12
  106.5 238.8 %reduce-scatter.5.cloned.1.call-start = ((), (), s32[]{:S(2)}) async-start(), calls=%async_computation.4 | async-start | bytes 5242880 | tf_op jit(solution)/shard_map/reduce_scatter | solution.py:78
  254.3 91.1 %copy-start.10 = (bf16[128,128]{1,0:T(8,128)(2,1)S(1)}, bf16[128,128]{1,0:T(8,128)(2,1)}, u32[]{:S(2)}) copy-start(bf16[128,128]{1,0:T(8,128)(2,1)} %param.23) | copy-start | bytes 98308
Sparse Core Ops, SparseCore 0:
  42.9 53.2 all-gather.2
  106.6 115.0 reduce-scatter.2
  257.7 87.5 reduce-scatter.4
